TPU v7x, 32 devices: a whole 2x2x4 slice. The times are simulated.
32 devices in a mesh: row: 8 (over y, x, core), col: 4 (over z).
Axes of the slice: x: 2, y: 2, z: 4, core: 2. Of those that a mesh axis runs over, the one named last changes fastest.
Arguments:
- x_tiles: float32 [64, 4096], P(('row', 'col')), may hold values from -6 to 6
- ham_tiles: float32 [2048, 4096], P(('row', 'col')), may hold values from -0.125 to 0.125
- tile_rows: int32 [2048], P(('row', 'col')), may hold values from 0 to 7, as said below
- tile_cols: int32 [2048], P(('row', 'col')), may hold values from 0 to 15, as said below
- tile_count: int32 [32], P(('row', 'col')), may hold values from 0 to 64, as said below
Outputs:
- product: float32 [64, 4096], P(('row', 'col'))
Inputs may be any that keep to these rules, and one draw needn't show every extreme that they name: For device d, its first tile_count[d] slots hold distinct positions (tile_rows, tile_cols) whose global tile row is at most the global tile column; the other slots are padding with indices in range. `tile_cols`: see tile_rows. `tile_count`: at most 64; equal to 64 on every device of row index 0.
All inputs are finite; a program needn't handle non-finite values.
Results may differ from a plain program's by a relative error of at most 0.0003.
Values sent between devices are 32-bit elements; how exact they have to be, the bound alone decides.
A program may use at most 128 MiB of HBM per device.

v0:
```python
import jax
import jax.numpy as jnp
from jax import lax
from jax.sharding import PartitionSpec as P

TILE = 64
VECS = 64


def shards(x_tiles, ham_tiles, tile_rows, tile_cols, tile_count):
    slots = ham_tiles.shape[0]
    width = x_tiles.shape[1]
    live = (jnp.arange(slots) < tile_count[0]).astype(jnp.float32)
    tiles = ham_tiles.reshape(slots, TILE, TILE)
    segment = lax.all_gather(x_tiles, "col", axis=0, tiled=True)
    piece = lax.all_gather(x_tiles, "row", axis=0, tiled=True)
    inside = (tile_cols >= 0) & (tile_cols < piece.shape[0])
    picked = jnp.take(piece, jnp.clip(tile_cols, 0, piece.shape[0] - 1), axis=0)
    far = jnp.where(inside[:, None], picked, 0.0)
    near = jnp.take(segment, tile_rows, axis=0)
    forward = jnp.einsum(
        "sij,sjk->sik", tiles, far.reshape(slots, TILE, VECS), precision=lax.Precision.HIGHEST
    )
    backward = jnp.einsum(
        "sji,sjk->sik", tiles, near.reshape(slots, TILE, VECS), precision=lax.Precision.HIGHEST
    )
    forward = forward.reshape(slots, width)
    backward = backward.reshape(slots, width)
    own_rows = x_tiles.shape[0]
    picks = (tile_rows[None, :] == jnp.arange(lax.axis_size("col") * own_rows)[:, None]).astype(
        jnp.float32
    ) * live[None, :]
    upper = lax.psum_scatter(
        jnp.dot(
            picks, forward, precision=lax.Precision.HIGHEST, preferred_element_type=jnp.float32
        ),
        "col",
        scatter_dimension=0,
        tiled=True,
    )
    picks = (tile_cols[None, :] == jnp.arange(lax.axis_size("row") * own_rows)[:, None]).astype(
        jnp.float32
    ) * live[None, :]
    lower = lax.psum_scatter(
        jnp.dot(
            picks, backward, precision=lax.Precision.HIGHEST, preferred_element_type=jnp.float32
        ),
        "row",
        scatter_dimension=0,
        tiled=True,
    )
    return upper + lower


def solution(mesh):
    placed = (
        P(("row", "col"), None),
        P(("row", "col"), None),
        P(("row", "col")),
        P(("row", "col")),
        P(("row", "col")),
    )
    return jax.shard_map(
        shards, mesh=mesh, in_specs=placed, out_specs=P(("row", "col"), None), check_vma=False
    )
```

profile of v0, /device:TPU:0, one launch (start us, length us, event | category | flops | bytes accessed | tf_op | source)
XLA Modules:
  0.0 136.5 jit_solution(1923507035828550838)
XLA Ops:
  6.5 0.0 all-reduce.5.cloned.1.call-start
  6.5 0.7 compare_and_fusion.1
  7.2 11.0 %all-gather = f32[8,2,4096]{2,1,0:T(2,128)S(1)} all-gather(f32[1,2,4096]{2,1,0:T(2,128)} %bitcast.13), channel_id=1, replica_groups=mesh['row'=8,'col'=4] {'row'}, dimensions={0}, use_global_device_ids=true | all-gather | bytes 294912 | tf_op jit(solution)/shard_map/all_gather | solution.py:16
  18.2 0.2 reshape.68
  18.4 0.9 gather_fusion
  19.3 0.8 gather.13
  20.1 0.0 copy-start
  20.2 1.8 %copy.12 = f32[64,64,64]{1,2,0:T(8,128)} copy(f32[64,64,64]{2,1,0:T(8,128)S(1)} %gather.13) | data formatting | bytes 2097152 | tf_op jit(solution)/shard_map/jit(_take)/gather | solution.py:18
  22.0 0.0 copy-done
  22.0 0.8 reshape.46
  22.8 6.6 %fusion.5 = f32[64,64,64]{1,2,0:T(8,128)} fusion(f32[64,64,64]{2,1,0:T(8,128)S(1)} %reshape.46, f32[64,64,64]{1,2,0:T(8,128)} %copy.12, pred[64]{0:T(512)(128)(4,1)S(1)} %get-tuple-element.5, pred[64]{0:T(512)(128)(4,1)S(1)} %get-tuple-element.7), kind=kOutput, calls=%fused_computation.7 | convolution fusion | flops 201850880 | bytes 3145856 | tf_op jit(solution)/shard_map/sij,sjk->sik/dot_general | solution.py:21
  29.4 2.9 %copy.13 = f32[64,64,64]{2,1,0:T(8,128)} copy(f32[64,64,64]{1,2,0:T(8,128)} %fusion.5) | data formatting | bytes 2097152 | tf_op jit(solution)/shard_map/sij,sjk->sik/dot_general | solution.py:21
  32.3 0.0 copy-start.3
  32.3 0.0 copy-start.1
  32.3 2.2 %reshape.47 = f32[64,4096]{1,0:T(8,128)S(1)} reshape(f32[64,64,64]{2,1,0:T(8,128)} %copy.13) | data formatting | bytes 2097152 | tf_op jit(solution)/shard_map/reshape | solution.py:27
  35.1 0.0 copy-done.3
  35.1 1.3 fusion.22
  36.4 0.0 all-reduce.5.cloned.1.call-update
  36.4 0.0 all-reduce.7.cloned.1.call-start
  36.5 0.0 copy-done.1
  36.5 14.0 %all-gather.1 = f32[4,2,4096]{2,1,0:T(2,128)S(1)} all-gather(f32[1,2,4096]{2,1,0:T(2,128)S(1)} %bitcast.14), channel_id=1, replica_groups=mesh['row'=8,'col'=4] {'col'}, dimensions={0}, use_global_device_ids=true | all-gather | bytes 163840 | tf_op jit(solution)/shard_map/all_gather | solution.py:15
  50.4 0.1 reshape.70
  50.6 0.9 gather_fusion.1
  51.5 2.1 %gather.15 = f32[64,64,64]{2,1,0:T(8,128)} reshape(f32[64,4096]{1,0:T(8,128)S(1)} %gather_fusion.1) | data formatting | bytes 2097152 | tf_op jit(solution)/shard_map/jit(_take)/gather | solution.py:20
  53.6 2.9 %copy.14 = f32[64,64,64]{1,2,0:T(8,128)} copy(f32[64,64,64]{2,1,0:T(8,128)} %gather.15) | data formatting | bytes 2097152 | tf_op jit(solution)/shard_map/jit(_take)/gather | solution.py:20
  56.6 5.2 %fusion.8 = f32[64,64,64]{1,2,0:T(8,128)} fusion(f32[64,64,64]{2,1,0:T(8,128)S(1)} %reshape.46, f32[64,64,64]{1,2,0:T(8,128)} %copy.14, pred[64]{0:T(512)(128)(4,1)S(1)} %compare_and_fusion), kind=kOutput, calls=%fused_computation.8 | convolution fusion | flops 201588736 | bytes 3145792 | tf_op jit(solution)/shard_map/sji,sjk->sik/dot_general | solution.py:24
  61.8 1.9 %copy.15 = f32[64,64,64]{2,1,0:T(8,128)S(1)} copy(f32[64,64,64]{1,2,0:T(8,128)} %fusion.8) | data formatting | bytes 2097152 | tf_op jit(solution)/shard_map/sji,sjk->sik/dot_general | solution.py:24
  63.7 0.0 copy-start.2
  63.7 0.0 copy-start.5
  63.7 0.0 copy-start.4
  63.8 0.7 reshape.48
  64.4 0.0 copy-done.2
  64.4 1.3 fusion.17
  65.7 0.0 all-reduce.7.cloned.1.call-update
  65.8 0.0 copy-done.5
  65.8 0.6 dynamic-slice
  66.4 0.0 copy-done.4
  66.4 0.6 dynamic-slice.2
  68.2 3.3 %all-reduce.5.cloned.1.call-done = f32[8,4096]{1,0:T(8,128)} async-done(((f32[8,4096]{1,0:T(8,128)}), f32[8,4096]{1,0:T(8,128)}) %all-reduce.5.cloned.1.call-update) | async-done | bytes 131088
  71.5 56.6 %all-reduce.7.cloned.1.call-done = f32[16,4096]{1,0:T(8,128)} async-done(((f32[16,4096]{1,0:T(8,128)}), f32[16,4096]{1,0:T(8,128)}) %all-reduce.7.cloned.1.call-update) | async-done | bytes 262160
  128.1 1.6 %dynamic-slice_add_fusion = f32[2,4096]{1,0:T(2,128)} fusion(f32[16,4096]{1,0:T(8,128)} %all-reduce.7.cloned.1.call-done, u32[]{:T(128)S(6)} %multiply.3, f32[8,4096]{1,0:T(8,128)} %all-reduce.5.cloned.1.call-done, u32[]{:T(128)S(6)} %multiply.1), kind=kLoop, calls=%fused_computation.15 | loop fusion | flops 8192 | bytes 98312 | tf_op jit(solution)/shard_map/add | solution.py:52
  (5 shorter events, 0.0 us)
Async XLA Ops:
  6.5 65.0 %all-reduce.5.cloned.1.call-start = ((), (), s32[]{:S(2)}) async-start(), calls=%async_computation | async-start | bytes 262144
  20.1 1.8 %copy-start = (f32[64,4096]{1,0:T(8,128)S(1)}, f32[64,4096]{1,0:T(8,128)}, u32[]{:S(2)}) copy-start(f32[64,4096]{1,0:T(8,128)} %param.6) | copy-start | bytes 3145732
  32.3 2.8 %copy-start.3 = (s32[64]{0:T(128)S(1)}, s32[64]{0:T(128)}, u32[]{:S(2)}) copy-start(s32[64]{0:T(128)} %param.7) | copy-start | bytes 772
  32.3 4.2 %copy-start.1 = (f32[2,4096]{1,0:T(2,128)S(1)}, f32[2,4096]{1,0:T(2,128)}, u32[]{:S(2)}) copy-start(f32[2,4096]{1,0:T(2,128)} %param.5) | copy-start | bytes 98308
  36.4 91.7 %all-reduce.7.cloned.1.call-start = ((), (), s32[]{:S(2)}) async-start(), calls=%async_computation.1 | async-start | bytes 524288
  63.7 0.7 copy-start.2
  63.7 2.0 %copy-start.5 = (u32[32]{0:T(128)S(1)}, u32[32]{0:T(128)}, u32[]{:S(2)}) copy-start(u32[32]{0:T(128)} %constant.42) | copy-start | bytes 388
  63.7 2.6 %copy-start.4 = (u32[32]{0:T(128)S(1)}, u32[32]{0:T(128)}, u32[]{:S(2)}) copy-start(u32[32]{0:T(128)} %constant.46) | copy-start | bytes 388
Sparse Core Ops, SparseCore 0:
  36.5 34.9 all-reduce.4
  74.8 53.1 all-reduce.6
where the time goes:
time: 137 us
  waiting for transfers between devices  59.9 us (44%)
  blocking collectives  24.9 us (18%)
  local copies, waits for them, and re-layouts  19.5 us (14%)
  between operations  15.5 us (11%)
  matrix products  14.3 us (10%)
  other arithmetic  2.3 us (2%)
    unnamed x4, waiting for transfers between devices  59.9 us
    all_gather x1, blocking collectives, shards(): segment = lax.all_gather(x_tiles, 'col', axis=0, tiled=True)  14 us
    all_gather x1, blocking collectives, shards(): piece = lax.all_gather(x_tiles, 'row', axis=0, tiled=True)  11 us
    dot_general x1, matrix products, shards(): jnp.einsum('sij,sjk->sik', tiles, far.reshape(slots, TILE, VECS), precisi...  6.57 us
    gather x3, local copies, waits for them, and re-layouts, shards(): near = jnp.take(segment, tile_rows, axis=0)  6.01 us
    dot_general x1, matrix products, shards(): jnp.einsum('sji,sjk->sik', tiles, near.reshape(slots, TILE, VECS), precis...  5.21 us
    gather x3, local copies, waits for them, and re-layouts, shards(): picked = jnp.take(piece, jnp.clip(tile_cols, 0, piece.shape[0] - 1), axis=0)  3.59 us
    dot_general x1, local copies, waits for them, and re-layouts, shards(): jnp.einsum('sij,sjk->sik', tiles, far.reshape(slots, TILE, VECS), precisi...  2.89 us
  transfers between devices with their start and end apart: 2, of which 2 were waited for; matrix products, arithmetic and copies ran while one was open for 12% of the time, Pallas kernels for 0%

commit v1 on v0

v1 whole, which is shorter than its diff:
```python
import functools

import jax
import jax.numpy as jnp
from jax import lax
from jax.experimental import pallas as pl
from jax.experimental.pallas import tpu as pltpu
from jax.sharding import PartitionSpec as P

TILE = 64
VECS = 64
LANES = 128
MESH = pl.DeviceIdType.MESH
F32 = jnp.float32
BF16 = jnp.bfloat16


def parts(value):
    high = value.astype(BF16)
    low = (value - high.astype(F32)).astype(BF16)
    return high, low


def kernel(
    n_row, n_col, tpd, slots,
    count_ref, rows_ref, cols_ref, x_ref, ham_ref, out_ref,
    ham, rows, cols, placed, m_high, m_low, far, near, stage, weights, near_t,
    up_own, up_got, low_own, low_got, turned,
    local_sems, far_send, far_recv, near_send, near_recv,
    up_send, up_recv, low_send, low_recv,
):
    r, c = lax.axis_index("row"), lax.axis_index("col")
    a_tiles, b_tiles = n_col * tpd, n_row * tpd
    positions = a_tiles * b_tiles
    packed = TILE * VECS // LANES
    wide = tpd * LANES

    def row_peer(k):
        return (lax.rem(r + k, n_row), c)

    def col_peer(k):
        return (r, lax.rem(c + k, n_col))

    get_x = pltpu.make_async_copy(x_ref, far.at[0], local_sems.at[0])
    get_near = pltpu.make_async_copy(x_ref, near.at[0], local_sems.at[1])
    get_rows = pltpu.make_async_copy(rows_ref, rows, local_sems.at[2])
    get_cols = pltpu.make_async_copy(cols_ref, cols, local_sems.at[3])
    get_ham = pltpu.make_async_copy(ham_ref, ham, local_sems.at[4])
    for copy in (get_x, get_near, get_rows, get_cols, get_ham):
        copy.start()

    barrier = pltpu.get_barrier_semaphore()
    for k in range(1, n_row):
        pl.semaphore_signal(barrier, inc=1, device_id=row_peer(k), device_id_type=MESH)
    for k in range(1, n_col):
        pl.semaphore_signal(barrier, inc=1, device_id=col_peer(k), device_id_type=MESH)
    pl.semaphore_wait(barrier, n_row + n_col - 2)

    get_x.wait()
    near_copies = []
    for k in range(1, n_col):
        copy = pltpu.make_async_remote_copy(
            src_ref=far.at[0], dst_ref=near.at[k],
            send_sem=near_send.at[k], recv_sem=near_recv.at[k],
            device_id=col_peer(n_col - k), device_id_type=MESH,
        )
        copy.start()
        near_copies.append(copy)
    far_copies = []
    for k in range(1, n_row):
        copy = pltpu.make_async_remote_copy(
            src_ref=far.at[0], dst_ref=far.at[k],
            send_sem=far_send.at[k], recv_sem=far_recv.at[k],
            device_id=row_peer(n_row - k), device_id_type=MESH,
        )
        copy.start()
        far_copies.append(copy)

    get_rows.wait()
    get_cols.wait()
    at_row = rows[...] - c * tpd
    at_row = jnp.where(at_row < 0, at_row + a_tiles, at_row)
    at_col = cols[...] - r * tpd
    at_col = jnp.where(at_col < 0, at_col + b_tiles, at_col)
    slot = lax.broadcasted_iota(jnp.int32, (1, slots), 1)
    place = jnp.where(slot < count_ref[0], at_row * b_tiles + at_col, -1)
    place = jnp.concatenate([place, place], axis=1)
    spot = lax.broadcasted_iota(jnp.int32, (positions, 2 * slots), 0)
    picks = jnp.where(spot == place, 1.0, 0.0).astype(BF16)

    get_ham.wait()
    for p in range(0, packed, 2):
        high, low = parts(ham[:, p * LANES:(p + 2) * LANES])
        both = jnp.concatenate([high, low], axis=0)
        put = jnp.dot(picks, both, preferred_element_type=F32)
        placed[p * positions:(p + 1) * positions, :] = put[:, :LANES]
        placed[(p + 1) * positions:(p + 2) * positions, :] = put[:, LANES:]

    def unfold(a, carry):
        for b in range(b_tiles):
            tile = placed[pl.ds(a * b_tiles + b, packed, stride=positions), :]
            high, low = parts(tile)
            at = pl.ds(pl.multiple_of(a * packed, packed), packed)
            m_high[at, b * LANES:(b + 1) * LANES] = high
            m_low[at, b * LANES:(b + 1) * LANES] = low
        return carry

    lax.fori_loop(0, a_tiles, unfold, 0)

    lane = lax.broadcasted_iota(jnp.int32, (TILE, LANES), 1)
    left = lane < TILE

    get_near.wait()
    for k in range(n_col):
        if k:
            near_copies[k - 1].wait_recv()
        for t in range(tpd):
            near_t[(k * tpd + t) * packed:(k * tpd + t + 1) * packed, :] = near[
                k, pl.ds(t, packed, stride=tpd), :
            ]
    high, low = parts(near_t[...].T)
    x_both = jnp.concatenate([high, low], axis=0)
    low_copies = []
    for k in list(range(1, n_row)) + [0]:
        block = slice(k * wide, (k + 1) * wide)
        first = jnp.dot(x_both, m_high[:, block], preferred_element_type=F32)
        second = jnp.dot(high, m_low[:, block], preferred_element_type=F32)
        total = first[:LANES] + first[LANES:] + second
        for t in range(0, tpd, 2):
            even = total[:, t * LANES:(t + 1) * LANES]
            odd = total[:, (t + 1) * LANES:(t + 2) * LANES]
            one = even[:TILE] + pltpu.roll(even[TILE:], TILE, 1)
            two = pltpu.roll(odd[:TILE], TILE, 1) + odd[TILE:]
            low_own[k, :, t * TILE:(t + 2) * TILE] = jnp.where(left, one, two)
        if k:
            copy = pltpu.make_async_remote_copy(
                src_ref=low_own.at[k], dst_ref=low_got.at[k],
                send_sem=low_send.at[k], recv_sem=low_recv.at[k],
                device_id=row_peer(k), device_id_type=MESH,
            )
            copy.start()
            low_copies.append(copy)

    half = left[:packed]
    for k in range(n_row):
        if k:
            far_copies[k - 1].wait_recv()
        for t in range(tpd):
            x = far[k, pl.ds(t, packed, stride=tpd), :]
            swapped = pltpu.roll(x, TILE, 1)
            stage[pl.ds(0, packed, stride=2), :] = jnp.where(half, x, 0.0)
            stage[pl.ds(1, packed, stride=2), :] = jnp.where(half, swapped, 0.0)
            stage[pl.ds(TILE, packed, stride=2), :] = jnp.where(half, 0.0, swapped)
            stage[pl.ds(TILE + 1, packed, stride=2), :] = jnp.where(half, 0.0, x)
            high, low = parts(stage[...])
            at = slice((k * tpd + t) * LANES, (k * tpd + t + 1) * LANES)
            weights[at, :LANES] = high
            weights[at, LANES:] = low
    first = jnp.dot(m_high[...], weights[...], preferred_element_type=F32)
    second = jnp.dot(m_low[...], weights[:, :LANES], preferred_element_type=F32)
    up_own[...] = first[:, :LANES] + first[:, LANES:] + second
    up_copies = []
    height = tpd * packed
    for k in range(1, n_col):
        copy = pltpu.make_async_remote_copy(
            src_ref=up_own.at[pl.ds(k * height, height)], dst_ref=up_got.at[k],
            send_sem=up_send.at[k], recv_sem=up_recv.at[k],
            device_id=col_peer(k), device_id_type=MESH,
        )
        copy.start()
        up_copies.append(copy)

    lower = low_own[0]
    for k in range(1, n_row):
        low_copies[k - 1].wait_recv()
        lower += low_got[k]
    turned[...] = jnp.concatenate([lower, lower], axis=0).T
    upper = up_own[:height, :]
    for k in range(1, n_col):
        up_copies[k - 1].wait_recv()
        upper += up_got[k]
    for t in range(tpd):
        even = turned[pl.ds(t * TILE, packed, stride=2), :]
        odd = turned[pl.ds(t * TILE + 1, packed, stride=2), :]
        out_ref[pl.ds(t, packed, stride=tpd), :] = (
            upper[t * packed:(t + 1) * packed] + jnp.where(half, even, odd)
        )
    for copy in near_copies + far_copies + low_copies + up_copies:
        copy.wait_send()


def solution(mesh):
    n_row, n_col = mesh.shape["row"], mesh.shape["col"]

    def shards(x_tiles, ham_tiles, tile_rows, tile_cols, tile_count):
        tpd, size = x_tiles.shape
        slots = ham_tiles.shape[0]
        packed = size // LANES
        a_tiles, b_tiles = n_col * tpd, n_row * tpd
        height = tpd * packed
        x = x_tiles.reshape(tpd, packed, LANES).transpose(1, 0, 2).reshape(height, LANES)
        anywhere = pl.BlockSpec(memory_space=pl.ANY)
        dma = pltpu.SemaphoreType.DMA
        out = pl.pallas_call(
            functools.partial(kernel, n_row, n_col, tpd, slots),
            out_shape=jax.ShapeDtypeStruct((height, LANES), F32),
            in_specs=[pl.BlockSpec(memory_space=pltpu.SMEM)] + [anywhere] * 4,
            out_specs=pl.BlockSpec(memory_space=pltpu.VMEM),
            scratch_shapes=[
                pltpu.VMEM((slots, size), F32),
                pltpu.VMEM((1, slots), jnp.int32),
                pltpu.VMEM((1, slots), jnp.int32),
                pltpu.VMEM((packed * a_tiles * b_tiles, LANES), F32),
                pltpu.VMEM((a_tiles * packed, b_tiles * LANES), BF16),
                pltpu.VMEM((a_tiles * packed, b_tiles * LANES), BF16),
                pltpu.VMEM((n_row, height, LANES), F32),
                pltpu.VMEM((n_col, height, LANES), F32),
                pltpu.VMEM((LANES, LANES), F32),
                pltpu.VMEM((b_tiles * LANES, 2 * LANES), BF16),
                pltpu.VMEM((a_tiles * packed, LANES), F32),
                pltpu.VMEM((a_tiles * packed, LANES), F32),
                pltpu.VMEM((n_col, height, LANES), F32),
                pltpu.VMEM((n_row, VECS, tpd * TILE), F32),
                pltpu.VMEM((n_row, VECS, tpd * TILE), F32),
                pltpu.VMEM((tpd * TILE, LANES), F32),
                dma((5,)),
                dma((n_row,)), dma((n_row,)), dma((n_col,)), dma((n_col,)),
                dma((n_col,)), dma((n_col,)), dma((n_row,)), dma((n_row,)),
            ],
            compiler_params=pltpu.CompilerParams(
                collective_id=0, has_side_effects=True, vmem_limit_bytes=48 * 1024 * 1024
            ),
        )(
            tile_count, tile_rows.reshape(1, slots), tile_cols.reshape(1, slots), x, ham_tiles
        )
        return out.reshape(packed, tpd, LANES).transpose(1, 0, 2).reshape(tpd, size)

    placed = (
        P(("row", "col"), None),
        P(("row", "col"), None),
        P(("row", "col")),
        P(("row", "col")),
        P(("row", "col")),
    )
    return jax.shard_map(
        shards, mesh=mesh, in_specs=placed, out_specs=P(("row", "col"), None), check_vma=False
    )
```

time: 137 us -> 22.2 us (0.16)
  waiting for transfers between devices: 59.9 us -> 0 us
  blocking collectives: 24.9 us -> 0 us
  Pallas kernels: 0 us -> 18 us
  local copies, waits for them, and re-layouts: 19.5 us -> 3.25 us
  between operations: 15.5 us -> 0.68 us
  matrix products: 14.3 us -> 0 us
  other arithmetic: 2.3 us -> 0 us
    unnamed x4 -> x0, waiting for transfers between devices: 59.9 us -> none
    all_gather x2 -> x0, blocking collectives: 24.9 us -> none  [the longest x1 14 us: shards(): segment = lax.all_gather(x_tiles, 'col', axis=0, tiled=True)]
    pallas_call x0 -> x1, Pallas kernels: none -> 18 us  [shards(): pl.pallas_call(functools.partial(kernel, n_row, n_col, tpd, slots), out_s...]
    dot_general x4 -> x0, matrix products: 14.3 us -> none  [the longest x1 6.57 us: shards(): jnp.einsum('sij,sjk->sik', tiles, far.reshape(slots, TILE, VECS), precisi...]
    gather x6 -> x0, local copies, waits for them, and re-layouts: 9.6 us -> none  [the longest x3 6.01 us: shards(): near = jnp.take(segment, tile_rows, axis=0)]
    dot_general x2 -> x0, local copies, waits for them, and re-layouts: 4.81 us -> none  [the longest x1 2.89 us: shards(): jnp.einsum('sij,sjk->sik', tiles, far.reshape(slots, TILE, VECS), precisi...]
    reshape x3 -> x0, local copies, waits for them, and re-layouts: 3.64 us -> none  [the longest x1 2.15 us: shards(): forward = forward.reshape(slots, width)]
    unnamed x16 -> x9, local copies, waits for them, and re-layouts: 1.48 us -> 3.25 us
  transfers between devices with their start and end apart: 2 -> 0, of which waited for: 2 -> 0; matrix products, arithmetic and copies ran while one was open for 12% -> 0% of each run, Pallas kernels for 0% -> 0%
where the time goes in v1:
time: 22.2 us; the launch traced here: 21.9 us
  Pallas kernels  18 us (81%)
  local copies, waits for them, and re-layouts  3.25 us (15%)
  between operations  0.68 us (3%)
    pallas_call x1, Pallas kernels, shards(): pl.pallas_call(functools.partial(kernel, n_row, n_col, tpd, slots), out_s...  18 us
    unnamed x9, local copies, waits for them, and re-layouts  3.25 us

profile of v1, /device:TPU:0, one launch (start us, length us, event | category | flops | bytes accessed | tf_op | source)
XLA Modules:
  0.0 21.9 jit_solution(8776571002108743616)
XLA Ops:
  0.7 0.0 copy-start.2
  0.7 0.0 copy-start.3
  0.7 0.6 %copy-done.2 = s32[64]{0:T(128)S(1)} copy-done((s32[64]{0:T(128)S(1)}, s32[64]{0:T(128)}, u32[]{:S(2)}) %copy-start.2) | copy-done | bytes 280
  1.3 0.0 copy-done.3
  1.3 0.0 copy-start
  1.3 1.2 %copy-done = f32[64,4096]{1,0:T(8,128)S(1)} copy-done((f32[64,4096]{1,0:T(8,128)S(1)}, f32[64,4096]{1,0:T(8,128)}, u32[]{:S(2)}) %copy-start) | copy-done | bytes 1048600
  2.5 0.0 copy-start.1
  2.6 0.8 %copy-done.1 = f32[2,4096]{1,0:T(2,128)S(1)} copy-done((f32[2,4096]{1,0:T(2,128)S(1)}, f32[2,4096]{1,0:T(2,128)}, u32[]{:S(2)}) %copy-start.1) | copy-done | bytes 32792
  3.3 18.0 %shard_map.55 = f32[64,128]{1,0:T(8,128)S(1)} custom-call(s32[1]{0:T(128)S(6)} %copy.9.count_ref, s32[1,64]{1,0:T(1,128)S(1)} %bitcast.14, s32[1,64]{1,0:T(1,128)S(1)} %bitcast.15, f32[64,128]{1,0:T(8,128)S(1)} %bitcast.13, f32[64,4096]{1,0:T(8,128)S(1)} %copy-done), custom_call_target="tpu_custom_call" | custom-call | tf_op jit(solution)/shard_map/pallas_call | solution.py:204
  21.3 0.6 %copy.10 = f32[2,4096]{1,0:T(2,128)} copy(f32[2,4096]{1,0:T(2,128)S(1)} %bitcast.12) | data formatting | bytes 65536
Async XLA Ops:
  0.7 0.7 %copy-start.2 = (s32[64]{0:T(128)S(1)}, s32[64]{0:T(128)}, u32[]{:S(2)}) copy-start(s32[64]{0:T(128)} %param.7) | copy-start | bytes 772
  0.7 0.7 %copy-start.3 = (s32[64]{0:T(128)S(1)}, s32[64]{0:T(128)}, u32[]{:S(2)}) copy-start(s32[64]{0:T(128)} %param.8) | copy-start | bytes 772
  1.3 1.2 %copy-start = (f32[64,4096]{1,0:T(8,128)S(1)}, f32[64,4096]{1,0:T(8,128)}, u32[]{:S(2)}) copy-start(f32[64,4096]{1,0:T(8,128)} %ham_ref.1) | copy-start | bytes 3145732
  2.5 0.8 %copy-start.1 = (f32[2,4096]{1,0:T(2,128)S(1)}, f32[2,4096]{1,0:T(2,128)}, u32[]{:S(2)}) copy-start(f32[2,4096]{1,0:T(2,128)} %param.5) | copy-start | bytes 98308

commit v2 on v1

--- a/solution.py
+++ b/solution.py
@@ -24,7 +24,7 @@
 def kernel(
     n_row, n_col, tpd, slots,
     count_ref, rows_ref, cols_ref, x_ref, ham_ref, out_ref,
-    ham, rows, cols, placed, m_high, m_low, far, near, stage, weights, near_t,
+    ham, count, rows, cols, placed, m_high, m_low, far, near, stage, weights, near_t,
     up_own, up_got, low_own, low_got, turned,
     local_sems, far_send, far_recv, near_send, near_recv,
     up_send, up_recv, low_send, low_recv,
@@ -45,8 +45,9 @@
     get_near = pltpu.make_async_copy(x_ref, near.at[0], local_sems.at[1])
     get_rows = pltpu.make_async_copy(rows_ref, rows, local_sems.at[2])
     get_cols = pltpu.make_async_copy(cols_ref, cols, local_sems.at[3])
-    get_ham = pltpu.make_async_copy(ham_ref, ham, local_sems.at[4])
-    for copy in (get_x, get_near, get_rows, get_cols, get_ham):
+    get_count = pltpu.make_async_copy(count_ref, count, local_sems.at[4])
+    get_ham = pltpu.make_async_copy(ham_ref, ham, local_sems.at[5])
+    for copy in (get_x, get_near, get_ham, get_rows, get_cols, get_count):
         copy.start()
 
     barrier = pltpu.get_barrier_semaphore()
@@ -78,12 +79,13 @@
 
     get_rows.wait()
     get_cols.wait()
+    get_count.wait()
     at_row = rows[...] - c * tpd
     at_row = jnp.where(at_row < 0, at_row + a_tiles, at_row)
     at_col = cols[...] - r * tpd
     at_col = jnp.where(at_col < 0, at_col + b_tiles, at_col)
     slot = lax.broadcasted_iota(jnp.int32, (1, slots), 1)
-    place = jnp.where(slot < count_ref[0], at_row * b_tiles + at_col, -1)
+    place = jnp.where(slot < count[...], at_row * b_tiles + at_col, -1)
     place = jnp.concatenate([place, place], axis=1)
     spot = lax.broadcasted_iota(jnp.int32, (positions, 2 * slots), 0)
     picks = jnp.where(spot == place, 1.0, 0.0).astype(BF16)
@@ -199,15 +201,16 @@
         a_tiles, b_tiles = n_col * tpd, n_row * tpd
         height = tpd * packed
         x = x_tiles.reshape(tpd, packed, LANES).transpose(1, 0, 2).reshape(height, LANES)
-        anywhere = pl.BlockSpec(memory_space=pl.ANY)
+        outside = pl.BlockSpec(memory_space=pltpu.HBM)
         dma = pltpu.SemaphoreType.DMA
         out = pl.pallas_call(
             functools.partial(kernel, n_row, n_col, tpd, slots),
             out_shape=jax.ShapeDtypeStruct((height, LANES), F32),
-            in_specs=[pl.BlockSpec(memory_space=pltpu.SMEM)] + [anywhere] * 4,
+            in_specs=[outside] * 5,
             out_specs=pl.BlockSpec(memory_space=pltpu.VMEM),
             scratch_shapes=[
                 pltpu.VMEM((slots, size), F32),
+                pltpu.VMEM((1, 1), jnp.int32),
                 pltpu.VMEM((1, slots), jnp.int32),
                 pltpu.VMEM((1, slots), jnp.int32),
                 pltpu.VMEM((packed * a_tiles * b_tiles, LANES), F32),
@@ -223,15 +226,15 @@
                 pltpu.VMEM((n_row, VECS, tpd * TILE), F32),
                 pltpu.VMEM((n_row, VECS, tpd * TILE), F32),
                 pltpu.VMEM((tpd * TILE, LANES), F32),
-                dma((5,)),
+                dma((6,)),
                 dma((n_row,)), dma((n_row,)), dma((n_col,)), dma((n_col,)),
                 dma((n_col,)), dma((n_col,)), dma((n_row,)), dma((n_row,)),
             ],
             compiler_params=pltpu.CompilerParams(
-                collective_id=0, has_side_effects=True, vmem_limit_bytes=48 * 1024 * 1024
+                collective_id=0, has_side_effects=True, vmem_limit_bytes=60 * 1024 * 1024
             ),
         )(
-            tile_count, tile_rows.reshape(1, slots), tile_cols.reshape(1, slots), x, ham_tiles
+            tile_count.reshape(1, 1), tile_rows.reshape(1, slots), tile_cols.reshape(1, slots), x, ham_tiles
         )
         return out.reshape(packed, tpd, LANES).transpose(1, 0, 2).reshape(tpd, size)
 

time: 22.2 us -> 20.7 us (0.932)
  local copies, waits for them, and re-layouts: 3.25 us -> 1.38 us
  Pallas kernels: 18 us -> 18.5 us
    unnamed x9 -> x1, local copies, waits for them, and re-layouts: 3.25 us -> 1.38 us
    pallas_call x1, Pallas kernels: 18 us -> 18.5 us  [shards(): pl.pallas_call(functools.partial(kernel, n_row, n_col, tpd, slots), out_s...]
where the time goes in v2:
time: 20.7 us; the launch traced here: 20.5 us
  Pallas kernels  18.5 us (89%)
  local copies, waits for them, and re-layouts  1.38 us (7%)
  between operations  0.66 us (3%)
    pallas_call x1, Pallas kernels, shards(): pl.pallas_call(functools.partial(kernel, n_row, n_col, tpd, slots), out_s...  18.5 us
    unnamed x1, local copies, waits for them, and re-layouts  1.38 us

profile of v2, /device:TPU:0, one launch (start us, length us, event | category | flops | bytes accessed | tf_op | source)
XLA Modules:
  0.0 20.5 jit_solution(16767467087994182058)
XLA Ops:
  0.7 18.5 %shard_map.55 = f32[64,128]{1,0:T(8,128)} custom-call(s32[1,1]{1,0:T(1,128)} %bitcast.13.count_ref, s32[1,64]{1,0:T(1,128)} %bitcast.16, s32[1,64]{1,0:T(1,128)} %bitcast.17, f32[64,128]{1,0:T(8,128)} %bitcast.15, f32[64,4096]{1,0:T(8,128)} %ham_ref.1), custom_call_target="tpu_custom_call" | custom-call | tf_op jit(solution)/shard_map/pallas_call | solution.py:206
  19.2 1.4 %copy.10 = f32[2,4096]{1,0:T(2,128)} copy(f32[2,4096]{1,0:T(2,128)} %bitcast.14) | data formatting | bytes 65536

commit v3 on v1

--- a/solution.py
+++ b/solution.py
@@ -34,26 +34,28 @@
     positions = a_tiles * b_tiles
     packed = TILE * VECS // LANES
     wide = tpd * LANES
+    order = sorted(range(1, n_row), key=lambda k: -min(k, n_row - k))
 
     def row_peer(k):
         return (lax.rem(r + k, n_row), c)
 
     def col_peer(k):
         return (r, lax.rem(c + k, n_col))
+
+    barrier = pltpu.get_barrier_semaphore()
+    for k in range(1, n_row):
+        pl.semaphore_signal(barrier, inc=1, device_id=row_peer(k), device_id_type=MESH)
+    for k in range(1, n_col):
+        pl.semaphore_signal(barrier, inc=1, device_id=col_peer(k), device_id_type=MESH)
 
     get_x = pltpu.make_async_copy(x_ref, far.at[0], local_sems.at[0])
     get_near = pltpu.make_async_copy(x_ref, near.at[0], local_sems.at[1])
     get_rows = pltpu.make_async_copy(rows_ref, rows, local_sems.at[2])
     get_cols = pltpu.make_async_copy(cols_ref, cols, local_sems.at[3])
     get_ham = pltpu.make_async_copy(ham_ref, ham, local_sems.at[4])
-    for copy in (get_x, get_near, get_rows, get_cols, get_ham):
-        copy.start()
-
-    barrier = pltpu.get_barrier_semaphore()
-    for k in range(1, n_row):
-        pl.semaphore_signal(barrier, inc=1, device_id=row_peer(k), device_id_type=MESH)
-    for k in range(1, n_col):
-        pl.semaphore_signal(barrier, inc=1, device_id=col_peer(k), device_id_type=MESH)
+    for copy in (get_x, get_near, get_ham, get_rows, get_cols):
+        copy.start()
+
     pl.semaphore_wait(barrier, n_row + n_col - 2)
 
     get_x.wait()
@@ -66,15 +68,15 @@
         )
         copy.start()
         near_copies.append(copy)
-    far_copies = []
-    for k in range(1, n_row):
+    far_copies = {}
+    for k in order:
         copy = pltpu.make_async_remote_copy(
             src_ref=far.at[0], dst_ref=far.at[k],
             send_sem=far_send.at[k], recv_sem=far_recv.at[k],
             device_id=row_peer(n_row - k), device_id_type=MESH,
         )
         copy.start()
-        far_copies.append(copy)
+        far_copies[k] = copy
 
     get_rows.wait()
     get_cols.wait()
@@ -110,6 +112,35 @@
     lane = lax.broadcasted_iota(jnp.int32, (TILE, LANES), 1)
     left = lane < TILE
 
+    half = left[:packed]
+    for k in range(n_row):
+        if k:
+            far_copies[k].wait_recv()
+        for t in range(tpd):
+            x = far[k, pl.ds(t, packed, stride=tpd), :]
+            swapped = pltpu.roll(x, TILE, 1)
+            stage[pl.ds(0, packed, stride=2), :] = jnp.where(half, x, 0.0)
+            stage[pl.ds(1, packed, stride=2), :] = jnp.where(half, swapped, 0.0)
+            stage[pl.ds(TILE, packed, stride=2), :] = jnp.where(half, 0.0, swapped)
+            stage[pl.ds(TILE + 1, packed, stride=2), :] = jnp.where(half, 0.0, x)
+            high, low = parts(stage[...])
+            at = slice((k * tpd + t) * LANES, (k * tpd + t + 1) * LANES)
+            weights[at, :LANES] = high
+            weights[at, LANES:] = low
+    first = jnp.dot(m_high[...], weights[...], preferred_element_type=F32)
+    second = jnp.dot(m_low[...], weights[:, :LANES], preferred_element_type=F32)
+    up_own[...] = first[:, :LANES] + first[:, LANES:] + second
+    up_copies = []
+    height = tpd * packed
+    for k in range(1, n_col):
+        copy = pltpu.make_async_remote_copy(
+            src_ref=up_own.at[pl.ds(k * height, height)], dst_ref=up_got.at[k],
+            send_sem=up_send.at[k], recv_sem=up_recv.at[k],
+            device_id=col_peer(k), device_id_type=MESH,
+        )
+        copy.start()
+        up_copies.append(copy)
+
     get_near.wait()
     for k in range(n_col):
         if k:
@@ -120,8 +151,8 @@
             ]
     high, low = parts(near_t[...].T)
     x_both = jnp.concatenate([high, low], axis=0)
-    low_copies = []
-    for k in list(range(1, n_row)) + [0]:
+    low_copies = {}
+    for k in order + [0]:
         block = slice(k * wide, (k + 1) * wide)
         first = jnp.dot(x_both, m_high[:, block], preferred_element_type=F32)
         second = jnp.dot(high, m_low[:, block], preferred_element_type=F32)
@@ -139,40 +170,11 @@
                 device_id=row_peer(k), device_id_type=MESH,
             )
             copy.start()
-            low_copies.append(copy)
-
-    half = left[:packed]
-    for k in range(n_row):
-        if k:
-            far_copies[k - 1].wait_recv()
-        for t in range(tpd):
-            x = far[k, pl.ds(t, packed, stride=tpd), :]
-            swapped = pltpu.roll(x, TILE, 1)
-            stage[pl.ds(0, packed, stride=2), :] = jnp.where(half, x, 0.0)
-            stage[pl.ds(1, packed, stride=2), :] = jnp.where(half, swapped, 0.0)
-            stage[pl.ds(TILE, packed, stride=2), :] = jnp.where(half, 0.0, swapped)
-            stage[pl.ds(TILE + 1, packed, stride=2), :] = jnp.where(half, 0.0, x)
-            high, low = parts(stage[...])
-            at = slice((k * tpd + t) * LANES, (k * tpd + t + 1) * LANES)
-            weights[at, :LANES] = high
-            weights[at, LANES:] = low
-    first = jnp.dot(m_high[...], weights[...], preferred_element_type=F32)
-    second = jnp.dot(m_low[...], weights[:, :LANES], preferred_element_type=F32)
-    up_own[...] = first[:, :LANES] + first[:, LANES:] + second
-    up_copies = []
-    height = tpd * packed
-    for k in range(1, n_col):
-        copy = pltpu.make_async_remote_copy(
-            src_ref=up_own.at[pl.ds(k * height, height)], dst_ref=up_got.at[k],
-            send_sem=up_send.at[k], recv_sem=up_recv.at[k],
-            device_id=col_peer(k), device_id_type=MESH,
-        )
-        copy.start()
-        up_copies.append(copy)
+            low_copies[k] = copy
 
     lower = low_own[0]
     for k in range(1, n_row):
-        low_copies[k - 1].wait_recv()
+        low_copies[k].wait_recv()
         lower += low_got[k]
     turned[...] = jnp.concatenate([lower, lower], axis=0).T
     upper = up_own[:height, :]
@@ -185,7 +187,7 @@
         out_ref[pl.ds(t, packed, stride=tpd), :] = (
             upper[t * packed:(t + 1) * packed] + jnp.where(half, even, odd)
         )
-    for copy in near_copies + far_copies + low_copies + up_copies:
+    for copy in near_copies + up_copies + list(far_copies.values()) + list(low_copies.values()):
         copy.wait_send()
 
 
@@ -199,12 +201,12 @@
         a_tiles, b_tiles = n_col * tpd, n_row * tpd
         height = tpd * packed
         x = x_tiles.reshape(tpd, packed, LANES).transpose(1, 0, 2).reshape(height, LANES)
-        anywhere = pl.BlockSpec(memory_space=pl.ANY)
+        outside = pl.BlockSpec(memory_space=pltpu.HBM)
         dma = pltpu.SemaphoreType.DMA
         out = pl.pallas_call(
             functools.partial(kernel, n_row, n_col, tpd, slots),
-            out_shape=jax.ShapeDtypeStruct((height, LANES), F32),
-            in_specs=[pl.BlockSpec(memory_space=pltpu.SMEM)] + [anywhere] * 4,
+            out_shape=pltpu.VMEM((height, LANES), F32),
+            in_specs=[pl.BlockSpec(memory_space=pltpu.SMEM)] + [outside] * 4,
             out_specs=pl.BlockSpec(memory_space=pltpu.VMEM),
             scratch_shapes=[
                 pltpu.VMEM((slots, size), F32),
@@ -228,7 +230,7 @@
                 dma((n_col,)), dma((n_col,)), dma((n_row,)), dma((n_row,)),
             ],
             compiler_params=pltpu.CompilerParams(
-                collective_id=0, has_side_effects=True, vmem_limit_bytes=48 * 1024 * 1024
+                collective_id=0, has_side_effects=True, vmem_limit_bytes=60 * 1024 * 1024
             ),
         )(
             tile_count, tile_rows.reshape(1, slots), tile_cols.reshape(1, slots), x, ham_tiles

time: 22.2 us -> 19.2 us (0.86)
  local copies, waits for them, and re-layouts: 3.25 us -> 0.62 us
    unnamed x9 -> x1, local copies, waits for them, and re-layouts: 3.25 us -> 0.62 us
    pallas_call x1, Pallas kernels: 18 us -> 17.8 us  [shards(): pl.pallas_call(functools.partial(kernel, n_row, n_col, tpd, slots), out_s...]
where the time goes in v3:
time: 19.2 us; the launch traced here: 19 us
  Pallas kernels  17.8 us (93%)
  between operations  0.66 us (3%)
  local copies, waits for them, and re-layouts  0.62 us (3%)
    pallas_call x1, Pallas kernels, shards(): pl.pallas_call(functools.partial(kernel, n_row, n_col, tpd, slots), out_s...  17.8 us
    unnamed x1, local copies, waits for them, and re-layouts  0.62 us

profile of v3, /device:TPU:0, one launch (start us, length us, event | category | flops | bytes accessed | tf_op | source)
XLA Modules:
  0.0 19.0 jit_solution(15164756188410509943)
XLA Ops:
  0.7 17.8 %shard_map.55 = f32[64,128]{1,0:T(8,128)S(1)} custom-call(s32[1]{0:T(128)S(6)} %copy.10.count_ref, s32[1,64]{1,0:T(1,128)} %bitcast.14, s32[1,64]{1,0:T(1,128)} %bitcast.15, f32[64,128]{1,0:T(8,128)} %bitcast.13, f32[64,4096]{1,0:T(8,128)} %ham_ref.1), custom_call_target="tpu_custom_call" | custom-call | tf_op jit(solution)/shard_map/pallas_call | solution.py:206
  18.4 0.6 %copy.9 = f32[2,4096]{1,0:T(2,128)} copy(f32[2,4096]{1,0:T(2,128)S(1)} %bitcast.12) | data formatting | bytes 65536

commit v4 on v3

--- a/solution.py
+++ b/solution.py
@@ -113,7 +113,7 @@
     left = lane < TILE
 
     half = left[:packed]
-    for k in range(n_row):
+    for k in [0] + order[::-1]:
         if k:
             far_copies[k].wait_recv()
         for t in range(tpd):
@@ -127,11 +127,11 @@
             at = slice((k * tpd + t) * LANES, (k * tpd + t + 1) * LANES)
             weights[at, :LANES] = high
             weights[at, LANES:] = low
-    first = jnp.dot(m_high[...], weights[...], preferred_element_type=F32)
-    second = jnp.dot(m_low[...], weights[:, :LANES], preferred_element_type=F32)
-    up_own[...] = first[:, :LANES] + first[:, LANES:] + second
+    height = tpd * packed
+    first = jnp.dot(m_high[height:, :], weights[...], preferred_element_type=F32)
+    second = jnp.dot(m_low[height:, :], weights[:, :LANES], preferred_element_type=F32)
+    up_own[height:, :] = first[:, :LANES] + first[:, LANES:] + second
     up_copies = []
-    height = tpd * packed
     for k in range(1, n_col):
         copy = pltpu.make_async_remote_copy(
             src_ref=up_own.at[pl.ds(k * height, height)], dst_ref=up_got.at[k],
@@ -172,15 +172,19 @@
             copy.start()
             low_copies[k] = copy
 
+    first = jnp.dot(m_high[:height, :], weights[...], preferred_element_type=F32)
+    second = jnp.dot(m_low[:height, :], weights[:, :LANES], preferred_element_type=F32)
+    up_own[:height, :] = first[:, :LANES] + first[:, LANES:] + second
+
+    upper = up_own[:height, :]
+    for k in range(1, n_col):
+        up_copies[k - 1].wait_recv()
+        upper += up_got[k]
     lower = low_own[0]
     for k in range(1, n_row):
         low_copies[k].wait_recv()
         lower += low_got[k]
     turned[...] = jnp.concatenate([lower, lower], axis=0).T
-    upper = up_own[:height, :]
-    for k in range(1, n_col):
-        up_copies[k - 1].wait_recv()
-        upper += up_got[k]
     for t in range(tpd):
         even = turned[pl.ds(t * TILE, packed, stride=2), :]
         odd = turned[pl.ds(t * TILE + 1, packed, stride=2), :]

time: 19.2 us -> 19.2 us (level)
  no operation moved by 1% of the time
where the time goes in v4:
time: 19.2 us; the launch traced here: 19.1 us
  Pallas kernels  17.8 us (93%)
  between operations  0.66 us (3%)
  local copies, waits for them, and re-layouts  0.62 us (3%)
    pallas_call x1, Pallas kernels, shards(): pl.pallas_call(functools.partial(kernel, n_row, n_col, tpd, slots), out_s...  17.8 us
    unnamed x1, local copies, waits for them, and re-layouts  0.62 us

profile of v4, /device:TPU:0, one launch (start us, length us, event | category | flops | bytes accessed | tf_op | source)
XLA Modules:
  0.0 19.1 jit_solution(2602101647198724834)
XLA Ops:
  0.7 17.8 %shard_map.55 = f32[64,128]{1,0:T(8,128)S(1)} custom-call(s32[1]{0:T(128)S(6)} %copy.10.count_ref, s32[1,64]{1,0:T(1,128)} %bitcast.14, s32[1,64]{1,0:T(1,128)} %bitcast.15, f32[64,128]{1,0:T(8,128)} %bitcast.13, f32[64,4096]{1,0:T(8,128)} %ham_ref.1), custom_call_target="tpu_custom_call" | custom-call | tf_op jit(solution)/shard_map/pallas_call | solution.py:210
  18.4 0.6 %copy.9 = f32[2,4096]{1,0:T(2,128)} copy(f32[2,4096]{1,0:T(2,128)S(1)} %bitcast.12) | data formatting | bytes 65536
